TPU v7x, 32 devices: a whole 2x2x4 slice. The times are simulated.
32 devices in a mesh: planes: 8 (over z, x), rows: 4 (over y, core).
Axes of the slice: x: 2, y: 2, z: 4, core: 2. Of those that a mesh axis runs over, the one named last changes fastest.
Arguments:
- movie: bfloat16 [65536, 2048], P(('planes', 'rows')), may hold values from -6 to 6
- entry_tile: int32 [65536], P(('planes', 'rows')), may hold values from 0 to 2047
- entry_neuron: int32 [65536], P(('planes', 'rows')), may hold values from 0 to 24575, as said below
- entry_weights: bfloat16 [65536, 128], P(('planes', 'rows')), may hold values from 0 to 0.1796875
- intersection_self: float32 [24576, 768], P(('planes', 'rows'))
- intersection_prev: float32 [24576, 768], P(('planes', 'rows')), may hold values from -0.0625 to 0.0625
- intersection_next: float32 [24576, 768], P(('planes', 'rows')), may hold values from -0.0625 to 0.0625
- prev_traces: float32 [16, 24576], P(None, ('planes', 'rows')), may hold values from 0 to 2
Outputs:
- traces: float32 [16, 24576], P(None, ('planes', 'rows'))
Inputs may be any that keep to these rules, and one draw needn't show every extreme that they name: `entry_neuron`: the footprint tiles of one device come in groups of 128 consecutive entries; all entries of one group name neurons of one neuron block (neuron // 768); the first group of each device names the device's own block, and the groups of one device name distinct blocks.
All inputs are finite; a program needn't handle non-finite values.
Results may differ from a plain program's by a relative error of at most 0.0003.
Values sent between devices are 32-bit elements; how exact they have to be, the bound alone decides.
A program may use at most 192 MiB of HBM per device.

v0:
```python
import jax
import jax.numpy as jnp
from jax import lax
from jax.sharding import PartitionSpec as P

SWEEPS = 3


def from_behind(block, axis, distance):
    devices = range(lax.axis_size(axis))
    route = [(i - distance, i) for i in devices if i - distance in devices]
    return lax.ppermute(block, axis, route)


def local(
    movie,
    entry_tile,
    entry_neuron,
    entry_weights,
    intersection_self,
    intersection_prev,
    intersection_next,
    prev_traces,
):
    devices = lax.axis_size(("planes", "rows"))
    neur_dev = prev_traces.shape[1]
    frames = prev_traces.shape[0]
    entries = entry_tile.shape[0]
    voxels = entry_weights.shape[1]
    picked = movie[entry_tile].reshape(entries, frames, voxels)
    contrib = jnp.einsum("efv,ev->ef", picked, entry_weights, preferred_element_type=jnp.float32)
    partial_value = (
        jnp.zeros((frames, neur_dev * devices), jnp.float32).at[:, entry_neuron].add(contrib.T)
    )
    projected = lax.psum_scatter(partial_value, ("planes", "rows"), scatter_dimension=1, tiled=True)
    diagonal = jnp.diagonal(intersection_self)
    highest = lax.Precision.HIGHEST
    current = prev_traces
    for sweep in range(SWEEPS):
        before = from_behind(current, ("planes", "rows"), 1)
        after = from_behind(current, ("planes", "rows"), -1)
        coupled = jnp.dot(current, intersection_self, precision=highest)
        coupled = coupled + jnp.dot(before, intersection_prev, precision=highest)
        coupled = coupled + jnp.dot(after, intersection_next, precision=highest)
        current = jnp.maximum(current + (projected - coupled) / diagonal, 0.0)
    return current


def solution(mesh):
    return jax.shard_map(
        local,
        mesh=mesh,
        in_specs=(
            P(("planes", "rows"), None),
            P(("planes", "rows")),
            P(("planes", "rows")),
            P(("planes", "rows"), None),
            P(("planes", "rows"), None),
            P(("planes", "rows"), None),
            P(("planes", "rows"), None),
            P(None, ("planes", "rows")),
        ),
        out_specs=P(None, ("planes", "rows")),
        check_vma=False,
    )
```

profile of v0, /device:TPU:7, one launch (start us, length us, event | category | flops | bytes accessed | tf_op | source)
XLA Modules:
  0.0 204.8 jit_solution(3524266941219065645)
XLA Ops:
  7.4 20.8 %gather_fusion = bf16[2048,2048]{1,0:T(8,128)(2,1)} fusion(bf16[2048,2048]{1,0:T(8,128)(2,1)} %param.8, s32[2048]{0:T(1024)S(1)} %fusion.16), kind=kCustom, calls=%fused_computation | custom fusion | bytes 16785408 | tf_op jit(solution)/shard_map/gather | solution.py:30
  28.2 9.8 %copy.13 = bf16[256,8,16,128]{3,2,1,0:T(8,128)(2,1)} copy(bf16[256,8,16,128]{3,1,2,0:T(8,128)(2,1)} %bitcast.24) | data formatting | bytes 16777216
  38.0 7.8 %fusion.14 = f32[2048,1,16]{2,1,0:T(1,128)S(1)} fusion(bf16[2048,16,128]{2,1,0:T(8,128)(2,1)} %bitcast.25, bf16[2048,128,1]{1,0,2:T(8,128)(2,1)S(1)} %bitcast.27), kind=kOutput, calls=%fused_computation.23 | convolution fusion | flops 8388608 | bytes 9043968 | tf_op jit(solution)/shard_map/efv,ev->ef/dot_general | solution.py:31
  45.8 16.8 %scatter_custom_fusion = f32[16,24576]{0,1:T(8,128)} fusion(s32[2048]{0:T(1024)S(1)} %compare_select_fusion.1, f32[2048,16]{1,0:T(8,128)S(1)} %bitcast.26, f32[]{:T(128)} %constant.4.clone.1), kind=kCustom, calls=%fused_computation.3 | custom fusion | flops 32768 | bytes 1572868 | tf_op jit(solution)/shard_map/scatter-add | solution.py:33
  62.6 8.4 %copy.10 = f32[16,24576]{1,0:T(8,128)} copy(f32[16,24576]{0,1:T(8,128)} %scatter_custom_fusion) | data formatting | bytes 3145728 | tf_op jit(solution)/shard_map/scatter-add | solution.py:33
  71.0 3.7 %collective-permute-start = (f32[16,768]{1,0:T(8,128)S(1)}, f32[16,768]{1,0:T(8,128)S(1)}, u32[]{:S(2)}, u32[]{:S(2)}) collective-permute-start(f32[16,768]{1,0:T(8,128)S(1)} %copy-done.4), channel_id=1, source_target_pairs={{0,1},{1,2},{2,3},{3,4},{4,5},{5,6},{6,7},{7,8},{8,9},{9,10},{10,1... | collective-permute-start | bytes 147464 | tf_op jit(solution)/shard_map/ppermute | solution.py:12
  74.7 1.9 collective-permute-start.1
  76.7 1.2 fusion.17
  77.9 6.3 %gather_fusion.1 = f32[768]{0:T(1024)S(1)} fusion(f32[768,768]{1,0:T(8,128)S(1)} %copy-done, s32[768]{0:T(1024)S(1)} %or_reduce_fusion), kind=kCustom, calls=%fused_computation.1 | custom fusion | bytes 12288 | tf_op jit(solution)/shard_map/jit(diagonal)/cond/branch_0_fun/gather | solution.py:36
  84.2 2.9 %convolution_add_fusion.5 = f32[16,768]{1,0:T(8,128)S(1)} fusion(f32[16,768]{1,0:T(8,128)S(1)} %fusion.17, f32[16,768]{1,0:T(8,128)S(1)} %collective-permute-done, f32[768,768]{1,0:T(8,128)} %param.13), kind=kOutput, calls=%fused_computation.22 | convolution fusion | flops 113258496 | bytes 2506752 | tf_op jit(solution)/shard_map/dot_general | solution.py:43
  87.1 80.4 %reduce-scatter.2.cloned.1.call-done = f32[16,768]{1,0:T(8,128)} async-done(((f32[16,24576]{1,0:T(8,128)}), f32[16,768]{1,0:T(8,128)}) %reduce-scatter.2.cloned.1.call-update) | async-done | bytes 49168 | tf_op jit(solution)/shard_map/reduce_scatter | solution.py:35
  167.6 3.0 %fusion.13 = f32[16,768]{1,0:T(8,128)S(1)} fusion(f32[16,768]{1,0:T(8,128)S(1)} %copy-done.4, f32[16,768]{1,0:T(8,128)} %reduce-scatter.2.cloned.1.call-done, f32[16,768]{1,0:T(8,128)S(1)} %convolution_add_fusion.5, f32[16,768]{1,0:T(8,128)S(1)} %collective-permute-done.1, f32[768,768]{1,0:T(8,128)} %param.14, f32[768]{0:T(1024)S(1)} %gather_fusion.1), kind=kOutput, calls=%fused_computation.21 | convolution fusion | flops 113307648 | bytes 2608128 | tf_op jit(solution)/shard_map/dot_general | solution.py:44
  170.6 5.5 %collective-permute-start.2 = (f32[16,768]{1,0:T(8,128)S(1)}, f32[16,768]{1,0:T(8,128)S(1)}, u32[]{:S(2)}, u32[]{:S(2)}) collective-permute-start(f32[16,768]{1,0:T(8,128)S(1)} %fusion.13), channel_id=1, source_target_pairs={{0,1},{1,2},{2,3},{3,4},{4,5},{5,6},{6,7},{7,8},{8,9},{9,10},{10,1... | collective-permute-start | bytes 147464 | tf_op jit(solution)/shard_map/ppermute | solution.py:12
  176.1 1.2 fusion.18
  177.3 1.9 collective-permute-start.3
  179.3 1.2 convolution_add_fusion.3
  180.5 4.0 %collective-permute-done.3 = f32[16,768]{1,0:T(8,128)S(1)} collective-permute-done((f32[16,768]{1,0:T(8,128)S(1)}, f32[16,768]{1,0:T(8,128)S(1)}, u32[]{:S(2)}, u32[]{:S(2)}) %collective-permute-start.3) | collective-permute-done | bytes 49184 | tf_op jit(solution)/shard_map/ppermute | solution.py:12
  184.5 1.2 fusion.9
  185.8 1.9 collective-permute-start.4
  187.7 1.2 fusion.19
  188.9 2.6 %collective-permute-start.5 = (f32[16,768]{1,0:T(8,128)S(1)}, f32[16,768]{1,0:T(8,128)S(1)}, u32[]{:S(2)}, u32[]{:S(2)}) collective-permute-start(f32[16,768]{1,0:T(8,128)S(1)} %fusion.9), channel_id=1, source_target_pairs={{1,0},{2,1},{3,2},{4,3},{5,4},{6,5},{7,6},{8,7},{9,8},{10,9},{11,1... | collective-permute-start | bytes 147464 | tf_op jit(solution)/shard_map/ppermute | solution.py:12
  191.5 1.2 convolution_add_fusion.1
  192.8 3.3 %collective-permute-done.5 = f32[16,768]{1,0:T(8,128)S(1)} collective-permute-done((f32[16,768]{1,0:T(8,128)S(1)}, f32[16,768]{1,0:T(8,128)S(1)}, u32[]{:S(2)}, u32[]{:S(2)}) %collective-permute-start.5) | collective-permute-done | bytes 49184 | tf_op jit(solution)/shard_map/ppermute | solution.py:12
  196.1 1.8 fusion.5
  (23 shorter events, 0.9 us)
Async XLA Ops:
  6.5 70.1 %copy-start = (f32[768,768]{1,0:T(8,128)S(1)}, f32[768,768]{1,0:T(8,128)}, u32[]{:S(2)}) copy-start(f32[768,768]{1,0:T(8,128)} %param.12) | copy-start | bytes 7077892
  6.5 161.0 %reduce-scatter.2.cloned.1.call-start = ((), (), s32[]{:S(2)}) async-start(), calls=%async_computation.1 | async-start | bytes 1622016 | tf_op jit(solution)/shard_map/reduce_scatter | solution.py:35
  28.2 9.8 %copy-start.5 = (s32[2048]{0:T(1024)S(1)}, s32[2048]{0:T(1024)}, u32[]{:S(2)}) copy-start(s32[2048]{0:T(1024)} %param.10) | copy-start | bytes 24580
  28.2 9.8 %copy-start.6 = (bf16[2048,128]{1,0:T(8,128)(2,1)S(1)}, bf16[2048,128]{1,0:T(8,128)(2,1)}, u32[]{:S(2)}) copy-start(bf16[2048,128]{1,0:T(8,128)(2,1)} %param.11) | copy-start | bytes 1572868
  62.6 8.4 %copy-start.4 = (f32[16,768]{1,0:T(8,128)S(1)}, f32[16,768]{1,0:T(8,128)}, u32[]{:S(2)}) copy-start(f32[16,768]{1,0:T(8,128)} %param.15) | copy-start | bytes 147460
  71.0 13.2 %collective-permute-start = (f32[16,768]{1,0:T(8,128)S(1)}, f32[16,768]{1,0:T(8,128)S(1)}, u32[]{:S(2)}, u32[]{:S(2)}) collective-permute-start(f32[16,768]{1,0:T(8,128)S(1)} %copy-done.4), channel_id=1, source_target_pairs={{0,1},{1,2},{2,3},{3,4},{4,5},{5,6},{6,7},{7,8},{8,9},{9,10},{10,1... | collective-permute-start | bytes 147464 | tf_op jit(solution)/shard_map/ppermute | solution.py:12
  74.7 12.4 %collective-permute-start.1 = (f32[16,768]{1,0:T(8,128)S(1)}, f32[16,768]{1,0:T(8,128)S(1)}, u32[]{:S(2)}, u32[]{:S(2)}) collective-permute-start(f32[16,768]{1,0:T(8,128)S(1)} %copy-done.4), channel_id=1, source_target_pairs={{1,0},{2,1},{3,2},{4,3},{5,4},{6,5},{7,6},{8,7},{9,8},{10,9},{11,1... | collective-permute-start | bytes 147464 | tf_op jit(solution)/shard_map/ppermute | solution.py:12
  167.5 11.7 %copy-start.2 = (f32[768,768]{1,0:T(8,128)S(1)}, f32[768,768]{1,0:T(8,128)}, u32[]{:S(2)}) copy-start(f32[768,768]{1,0:T(8,128)} %param.13) | copy-start | bytes 7077892
  170.6 13.9 %copy-start.1 = (f32[768,768]{1,0:T(8,128)S(1)}, f32[768,768]{1,0:T(8,128)}, u32[]{:S(2)}) copy-start(f32[768,768]{1,0:T(8,128)} %param.14) | copy-start | bytes 7077892
  170.6 13.9 %copy-start.3 = (f32[16,768]{1,0:T(8,128)S(1)}, f32[16,768]{1,0:T(8,128)}, u32[]{:S(2)}) copy-start(f32[16,768]{1,0:T(8,128)} %reduce-scatter.2.cloned.1.call-done) | copy-start | bytes 147460
  170.6 8.6 %collective-permute-start.2 = (f32[16,768]{1,0:T(8,128)S(1)}, f32[16,768]{1,0:T(8,128)S(1)}, u32[]{:S(2)}, u32[]{:S(2)}) collective-permute-start(f32[16,768]{1,0:T(8,128)S(1)} %fusion.13), channel_id=1, source_target_pairs={{0,1},{1,2},{2,3},{3,4},{4,5},{5,6},{6,7},{7,8},{8,9},{9,10},{10,1... | collective-permute-start | bytes 147464 | tf_op jit(solution)/shard_map/ppermute | solution.py:12
  177.3 7.2 %collective-permute-start.3 = (f32[16,768]{1,0:T(8,128)S(1)}, f32[16,768]{1,0:T(8,128)S(1)}, u32[]{:S(2)}, u32[]{:S(2)}) collective-permute-start(f32[16,768]{1,0:T(8,128)S(1)} %fusion.13), channel_id=1, source_target_pairs={{1,0},{2,1},{3,2},{4,3},{5,4},{6,5},{7,6},{8,7},{9,8},{10,9},{11,1... | collective-permute-start | bytes 147464 | tf_op jit(solution)/shard_map/ppermute | solution.py:12
  185.8 5.8 %collective-permute-start.4 = (f32[16,768]{1,0:T(8,128)S(1)}, f32[16,768]{1,0:T(8,128)S(1)}, u32[]{:S(2)}, u32[]{:S(2)}) collective-permute-start(f32[16,768]{1,0:T(8,128)S(1)} %fusion.9), channel_id=1, source_target_pairs={{0,1},{1,2},{2,3},{3,4},{4,5},{5,6},{6,7},{7,8},{8,9},{9,10},{10,1... | collective-permute-start | bytes 147464 | tf_op jit(solution)/shard_map/ppermute | solution.py:12
  188.9 7.2 %collective-permute-start.5 = (f32[16,768]{1,0:T(8,128)S(1)}, f32[16,768]{1,0:T(8,128)S(1)}, u32[]{:S(2)}, u32[]{:S(2)}) collective-permute-start(f32[16,768]{1,0:T(8,128)S(1)} %fusion.9), channel_id=1, source_target_pairs={{1,0},{2,1},{3,2},{4,3},{5,4},{6,5},{7,6},{8,7},{9,8},{10,9},{11,1... | collective-permute-start | bytes 147464 | tf_op jit(solution)/shard_map/ppermute | solution.py:12
Sparse Core Ops, SparseCore 0:
  71.1 96.3 reduce-scatter.1
where the time goes:
time: 205 us
  waiting for transfers between devices  87.8 us (43%)
  local copies, waits for them, and re-layouts  45.4 us (22%)
  matrix products  22.9 us (11%)
  other arithmetic  17.7 us (9%)
  starting transfers between devices  17.5 us (9%)
  between operations  13.6 us (7%)
    reduce_scatter x1, waiting for transfers between devices, local(): lax.psum_scatter(partial_value, ('planes', 'rows'), scatter_dimension=1,...  80.4 us
    gather x1, local copies, waits for them, and re-layouts, local(): picked = movie[entry_tile].reshape(entries, frames, voxels)  20.8 us
    ppermute x6, starting transfers between devices, from_behind(): return lax.ppermute(block, axis, route)  17.5 us
    scatter-add x1, other arithmetic, local(): jnp.zeros((frames, neur_dev * devices), jnp.float32).at[:, entry_neuron]  16.8 us
    unnamed x15, local copies, waits for them, and re-layouts  9.85 us
    scatter-add x1, local copies, waits for them, and re-layouts, local(): jnp.zeros((frames, neur_dev * devices), jnp.float32).at[:, entry_neuron]  8.39 us
    dot_general x1, matrix products, local(): jnp.einsum('efv,ev->ef', picked, entry_weights, preferred_element_type=jn...  7.79 us
    ppermute x6, waiting for transfers between devices, from_behind(): return lax.ppermute(block, axis, route)  7.39 us
  transfers between devices with their start and end apart: 7, of which 3 were waited for; matrix products, arithmetic and copies ran while one was open for 7% of the time, Pallas kernels for 0%

commit v1 on v0

v1 whole, which is shorter than its diff:
```python
import functools

import jax
import jax.numpy as jnp
from jax import lax
from jax.experimental import pallas as pl
from jax.experimental.pallas import tpu as pltpu
from jax.sharding import PartitionSpec as P

SWEEPS = 3
LANES = 128
STEPS = 8
BATCH = 8
F32 = jnp.float32
BF16 = jnp.bfloat16
MESH = pl.DeviceIdType.MESH
NT = (((1,), (1,)), ((), ()))


def contrib_kernel(cap, neur_dev, tile_s, neuron_s, movie, weights, neuron_v, out, staged):
    step = pl.program_id(0)
    rows = movie.shape[0]
    frames = out.shape[1] - 1

    @pl.loop(0, rows // 16)
    def _(r):
        base = pl.multiple_of(r * 16, 16)
        for f in range(frames):
            x = movie[pl.ds(base, 16), f * LANES:(f + 1) * LANES].astype(F32)
            staged[pl.ds((step * rows + base) * frames + f, 16, stride=frames), :] = x

    @pl.when(step == pl.num_programs(0) - 1)
    def _():
        for d in range(out.shape[0]):
            out[d, :frames] = jnp.zeros((frames, LANES), F32)
            out[d, frames:] = jnp.full((1, LANES), -1.0, F32)
        lane = lax.broadcasted_iota(jnp.int32, (frames, LANES), 1)
        part = 32

        @pl.loop(0, weights.shape[0] // LANES)
        def _(c):
            first = pl.multiple_of(c * LANES, LANES)
            w = weights[pl.ds(first, LANES), :]
            acc = jnp.zeros((frames, LANES), F32)
            for p in range(0, LANES, part):
                picked = [
                    staged[pl.ds(pl.multiple_of(tile_s[first + p + i] * frames, frames), frames), :].astype(BF16)
                    for i in range(part)
                ]
                prod = lax.dot_general(jnp.concatenate(picked, axis=0), w, NT, preferred_element_type=F32)
                for i in range(part):
                    acc = jnp.where(lane == p + i, prod[i * frames:(i + 1) * frames], acc)
            names = neuron_v[pl.ds(c, 1), :].astype(F32)
            for q in range(0, LANES, cap):
                owner = neuron_s[first + q] // neur_dev
                out[owner, :frames] = acc
                out[owner, frames:] = names


def halves(x):
    hi = x.astype(BF16)
    return hi, (x - hi.astype(F32)).astype(BF16)


def sweep_kernel(
    n,
    n_rows,
    slots,
    self_h,
    prev_h,
    next_h,
    start,
    traces,
    landed,
    raw,
    high,
    low,
    diag,
    projected,
    current,
    before,
    after,
    raw_sem,
    own_sem,
    send_sem,
    recv_sem,
    near_send,
    near_recv,
):
    me = lax.axis_index("planes") * n_rows + lax.axis_index("rows")
    frames, neur_dev = start.shape

    def place(d):
        return (d // n_rows, lax.rem(d, n_rows))

    loads = [pltpu.make_async_copy(h, raw.at[i], raw_sem.at[i]) for i, h in enumerate((self_h, prev_h, next_h))]
    for load in loads:
        load.start()
    own = pltpu.make_async_copy(slots.at[me], landed.at[me], own_sem)
    own.start()

    barrier = pltpu.get_barrier_semaphore()

    @pl.loop(1, n)
    def _(off):
        pl.semaphore_signal(barrier, inc=1, device_id=place(lax.rem(me + off, n)), device_id_type=MESH)

    pl.semaphore_wait(barrier, n - 1)

    def to_next(src, k):
        return pltpu.make_async_remote_copy(
            src_ref=src, dst_ref=before.at[k], send_sem=near_send.at[0, k], recv_sem=near_recv.at[0, k],
            device_id=place(lax.rem(me + 1, n)), device_id_type=MESH)

    def to_prev(src, k):
        return pltpu.make_async_remote_copy(
            src_ref=src, dst_ref=after.at[k], send_sem=near_send.at[1, k], recv_sem=near_recv.at[1, k],
            device_id=place(lax.rem(me + n - 1, n)), device_id_type=MESH)

    def share(src, k):
        @pl.when(me < n - 1)
        def _():
            to_next(src, k).start()

        @pl.when(me > 0)
        def _():
            to_prev(src, k).start()

    def receive(src, k):
        @pl.when(me > 0)
        def _():
            to_next(src, k).wait_recv()

        @pl.when(me < n - 1)
        def _():
            to_prev(src, k).wait_recv()

        @pl.when(me == 0)
        def _():
            before[k] = jnp.zeros((frames, neur_dev), F32)

        @pl.when(me == n - 1)
        def _():
            after[k] = jnp.zeros((frames, neur_dev), F32)

    def sent(src, k):
        @pl.when(me < n - 1)
        def _():
            to_next(src, k).wait_send()

        @pl.when(me > 0)
        def _():
            to_prev(src, k).wait_send()

    share(start, 0)

    def slot_copy(off):
        d = lax.rem(me + off, n)
        return pltpu.make_async_remote_copy(
            src_ref=slots.at[d], dst_ref=landed.at[me], send_sem=send_sem.at[d], recv_sem=recv_sem.at[me],
            device_id=place(d), device_id_type=MESH)

    @pl.loop(1, n)
    def _(off):
        slot_copy(off).start()

    eye = lax.broadcasted_iota(jnp.int32, (LANES, LANES), 0) == lax.broadcasted_iota(jnp.int32, (LANES, LANES), 1)
    for m in range(3):
        loads[m].wait()
        if m == 0:
            for b in range(0, neur_dev, LANES):
                block = raw[0, b:b + LANES, b:b + LANES]
                diag[:, b:b + LANES] = jnp.sum(jnp.where(eye, block, 0.0), axis=0, keepdims=True)
                raw[0, b:b + LANES, b:b + LANES] = jnp.where(eye, 0.0, block)

        @pl.loop(0, neur_dev // 16)
        def _(r):
            rows = pl.ds(pl.multiple_of(r * 16, 16), 16)
            hi, lo = halves(raw[m, rows, :])
            high[m, rows, :] = hi
            low[m, rows, :] = lo

    def product(c, m):
        hi, lo = halves(c)
        both = jnp.dot(jnp.concatenate([hi, lo], axis=0), high[m], preferred_element_type=F32)
        small = jnp.dot(hi, low[m], preferred_element_type=F32)
        return both[:frames] + (both[frames:] + small)

    receive(start, 0)
    coupled = product(start[...], 0) + product(before[0], 1) + product(after[0], 2)

    projected[...] = jnp.zeros_like(projected)
    number = lax.broadcasted_iota(jnp.int32, (neur_dev, LANES), 0).astype(F32)
    shift = (me * neur_dev).astype(F32)
    own.wait()

    @pl.loop(0, n // BATCH)
    def _(b):
        hots, values = [], []
        for s in range(BATCH):
            off = b * BATCH + s
            source = lax.rem(me + n - off, n)

            @pl.when(off > 0)
            def _():
                pltpu.make_async_remote_copy(
                    src_ref=slots.at[source], dst_ref=landed.at[source], send_sem=send_sem.at[source],
                    recv_sem=recv_sem.at[source], device_id=place(source), device_id_type=MESH).wait_recv()

        for s in range(BATCH):
            source = lax.rem(me + n - (b * BATCH + s), n)
            names = landed[source, frames:] - shift
            hots.append(jnp.where(number == names, 1.0, 0.0).astype(BF16))
            values.append(jnp.concatenate(halves(landed[source, :frames]), axis=0))
        projected[...] += lax.dot_general(
            jnp.concatenate(values, axis=1), jnp.concatenate(hots, axis=1), NT, preferred_element_type=F32)

    total = projected[:frames] + projected[frames:]
    scale = diag[...]
    for k in range(1, SWEEPS):
        current[k - 1] = jnp.maximum((total - coupled) / scale, 0.0)
        share(current.at[k - 1], k)
        coupled = product(current[k - 1], 0)
        receive(current.at[k - 1], k)
        coupled = coupled + product(before[k], 1) + product(after[k], 2)
    traces[...] = jnp.maximum((total - coupled) / scale, 0.0)

    sent(start, 0)
    for k in range(1, SWEEPS):
        sent(current.at[k - 1], k)

    @pl.loop(1, n)
    def _(off):
        slot_copy(off).wait_send()


def local(
    movie,
    entry_tile,
    entry_neuron,
    entry_weights,
    intersection_self,
    intersection_prev,
    intersection_next,
    prev_traces,
):
    n_rows = lax.axis_size("rows")
    n = lax.axis_size("planes") * n_rows
    frames, neur_dev = prev_traces.shape
    entries = entry_tile.shape[0]
    tiles = movie.shape[0]
    cap = 2 * entries // n
    whole = pl.BlockSpec(memory_space=pltpu.VMEM)
    scalar = pl.BlockSpec(memory_space=pltpu.SMEM)
    anywhere = pl.BlockSpec(memory_space=pl.ANY)
    slots = pl.pallas_call(
        functools.partial(contrib_kernel, cap, neur_dev),
        grid=(STEPS,),
        in_specs=[
            scalar,
            scalar,
            pl.BlockSpec((tiles // STEPS, frames * LANES), lambda i: (i, 0)),
            whole,
            whole,
        ],
        out_specs=pl.BlockSpec((n, frames + 1, LANES), lambda i: (0, 0, 0)),
        out_shape=jax.ShapeDtypeStruct((n, frames + 1, LANES), F32),
        scratch_shapes=[pltpu.VMEM((tiles * frames, LANES), F32)],
        compiler_params=pltpu.CompilerParams(vmem_limit_bytes=40 * 2**20),
        name="contrib",
    )(entry_tile, entry_neuron, movie, entry_weights, entry_neuron.reshape(entries // LANES, LANES))
    return pl.pallas_call(
        functools.partial(sweep_kernel, n, n_rows),
        in_specs=[anywhere] * 4 + [whole],
        out_specs=whole,
        out_shape=jax.ShapeDtypeStruct((frames, neur_dev), F32),
        scratch_shapes=[
            pltpu.VMEM((n, frames + 1, LANES), F32),
            pltpu.VMEM((3, neur_dev, neur_dev), F32),
            pltpu.VMEM((3, neur_dev, neur_dev), BF16),
            pltpu.VMEM((3, neur_dev, neur_dev), BF16),
            pltpu.VMEM((1, neur_dev), F32),
            pltpu.VMEM((2 * frames, neur_dev), F32),
            pltpu.VMEM((SWEEPS - 1, frames, neur_dev), F32),
            pltpu.VMEM((SWEEPS, frames, neur_dev), F32),
            pltpu.VMEM((SWEEPS, frames, neur_dev), F32),
            pltpu.SemaphoreType.DMA((3,)),
            pltpu.SemaphoreType.DMA,
            pltpu.SemaphoreType.DMA((n,)),
            pltpu.SemaphoreType.DMA((n,)),
            pltpu.SemaphoreType.DMA((2, SWEEPS)),
            pltpu.SemaphoreType.DMA((2, SWEEPS)),
        ],
        compiler_params=pltpu.CompilerParams(
            vmem_limit_bytes=40 * 2**20, collective_id=0, has_side_effects=True),
        name="sweeps",
    )(slots, intersection_self, intersection_prev, intersection_next, prev_traces)


def solution(mesh):
    spread = ("planes", "rows")
    return jax.shard_map(
        local,
        mesh=mesh,
        in_specs=(
            P(spread, None),
            P(spread),
            P(spread),
            P(spread, None),
            P(spread, None),
            P(spread, None),
            P(spread, None),
            P(None, spread),
        ),
        out_specs=P(None, spread),
        check_vma=False,
    )
```

time: 205 us -> 44.1 us (0.22)
  waiting for transfers between devices: 87.8 us -> 0 us
  local copies, waits for them, and re-layouts: 45.4 us -> 6.45 us
  Pallas kernels: 0 us -> 37.4 us
  matrix products: 22.9 us -> 0 us
  other arithmetic: 17.7 us -> 0 us
  starting transfers between devices: 17.5 us -> 0 us
  between operations: 13.6 us -> 0.06 us
    reduce_scatter x1 -> x0, waiting for transfers between devices: 80.4 us -> none  [local(): lax.psum_scatter(partial_value, ('planes', 'rows'), scatter_dimension=1,...]
    pallas_call x0 -> x2, Pallas kernels: none -> 37.4 us  [the longest x1 25.7 us: local(): pl.pallas_call(functools.partial(sweep_kernel, n, n_rows), in_specs=[anyw...]
    gather x2 -> x0, local copies, waits for them, and re-layouts: 27.1 us -> none  [the longest x1 20.8 us: local(): picked = movie[entry_tile].reshape(entries, frames, voxels)]
    dot_general x10 -> x0, matrix products: 22.9 us -> none  [the longest x1 7.79 us: local(): jnp.einsum('efv,ev->ef', picked, entry_weights, preferred_element_type=jn...]
    ppermute x6 -> x0, starting transfers between devices: 17.5 us -> none  [from_behind(): return lax.ppermute(block, axis, route)]
    scatter-add x1 -> x0, other arithmetic: 16.8 us -> none  [local(): jnp.zeros((frames, neur_dev * devices), jnp.float32).at[:, entry_neuron]]
    scatter-add x1 -> x0, local copies, waits for them, and re-layouts: 8.39 us -> none  [local(): jnp.zeros((frames, neur_dev * devices), jnp.float32).at[:, entry_neuron]]
    ppermute x6 -> x0, waiting for transfers between devices: 7.39 us -> none  [from_behind(): return lax.ppermute(block, axis, route)]
  transfers between devices with their start and end apart: 7 -> 0, of which waited for: 3 -> 0; matrix products, arithmetic and copies ran while one was open for 7% -> 0% of each run, Pallas kernels for 0% -> 0%
where the time goes in v1:
time: 44.1 us; the launch traced here: 43.9 us
  Pallas kernels  37.4 us (85%)
  local copies, waits for them, and re-layouts  6.45 us (15%)
    pallas_call x1, Pallas kernels, local(): pl.pallas_call(functools.partial(sweep_kernel, n, n_rows), in_specs=[anyw...  25.7 us
    pallas_call x1, Pallas kernels, local(): pl.pallas_call(functools.partial(contrib_kernel, cap, neur_dev), grid=(ST...  11.6 us
    unnamed x17, local copies, waits for them, and re-layouts  6.45 us

profile of v1, /device:TPU:7, one launch (start us, length us, event | category | flops | bytes accessed | tf_op | source)
XLA Modules:
  0.0 43.9 jit_solution(17163536454177542789)
XLA Ops:
  0.0 0.0 copy-start
  0.0 3.4 %copy-done = bf16[2048,2048]{1,0:T(8,128)(2,1)S(1)} copy-done((bf16[2048,2048]{1,0:T(8,128)(2,1)S(1)}, bf16[2048,2048]{1,0:T(8,128)(2,1)}, u32[]{:S(2)}) %copy-start) | copy-done | bytes 8388632
  3.4 0.0 copy-start.4
  3.4 1.0 %copy-done.4 = bf16[2048,128]{1,0:T(8,128)(2,1)S(1)} copy-done((bf16[2048,128]{1,0:T(8,128)(2,1)S(1)}, bf16[2048,128]{1,0:T(8,128)(2,1)}, u32[]{:S(2)}) %copy-start.4) | copy-done | bytes 524312
  4.4 0.0 copy-start.6
  4.4 0.7 %copy-done.6 = s32[2048]{0:T(1024)S(1)} copy-done((s32[2048]{0:T(1024)S(1)}, s32[2048]{0:T(1024)}, u32[]{:S(2)}) %copy-start.6) | copy-done | bytes 8216
  5.1 0.0 copy-start.7
  5.1 0.7 %copy-done.7 = s32[2048]{0:T(1024)S(1)} copy-done((s32[2048]{0:T(1024)S(1)}, s32[2048]{0:T(1024)}, u32[]{:S(2)}) %copy-start.7) | copy-done | bytes 8216
  5.8 0.0 copy-start.1
  5.8 0.0 copy-start.2
  5.8 0.0 copy-start.3
  5.8 0.0 copy-start.5
  5.8 11.6 %contrib.1.slots = f32[32,17,128]{2,1,0:T(8,128)S(1)} custom-call(s32[2048]{0:T(1024)S(1)} %copy-done.7, s32[2048]{0:T(1024)S(1)} %copy-done.6, bf16[2048,2048]{1,0:T(8,128)(2,1)S(1)} %copy-done, bf16[2048,128]{1,0:T(8,128)(2,1)S(1)} %copy-done.4, s32[16,128]{1,0:T(8,128)S(1)} %bitcast.1), custom_call_target="tpu_custom_call" | custom-call | tf_op jit(solution)/shard_map/contrib/pallas_call | solution.py:256
  17.5 0.0 copy-done.1
  17.5 0.0 copy-done.2
  17.5 0.0 copy-done.3
  17.5 0.0 copy-done.5
  17.5 25.7 %sweeps.1 = f32[16,768]{1,0:T(8,128)S(1)} custom-call(f32[32,17,128]{2,1,0:T(8,128)S(1)} %contrib.1.slots, f32[768,768]{1,0:T(8,128)S(1)} %copy-done.1, f32[768,768]{1,0:T(8,128)S(1)} %copy-done.2, f32[768,768]{1,0:T(8,128)S(1)} %copy-done.3, f32[16,768]{1,0:T(8,128)S(1)} %copy-done.5), custom_call_target="tpu_custom_call" | custom-call | tf_op jit(solution)/shard_map/sweeps/pallas_call | solution.py:272
  43.2 0.6 %copy.10 = f32[16,768]{1,0:T(8,128)} copy(f32[16,768]{1,0:T(8,128)S(1)} %sweeps.1) | data formatting | bytes 98304
Async XLA Ops:
  0.0 3.4 %copy-start = (bf16[2048,2048]{1,0:T(8,128)(2,1)S(1)}, bf16[2048,2048]{1,0:T(8,128)(2,1)}, u32[]{:S(2)}) copy-start(bf16[2048,2048]{1,0:T(8,128)(2,1)} %movie.1) | copy-start | bytes 25165828
  3.4 1.0 %copy-start.4 = (bf16[2048,128]{1,0:T(8,128)(2,1)S(1)}, bf16[2048,128]{1,0:T(8,128)(2,1)}, u32[]{:S(2)}) copy-start(bf16[2048,128]{1,0:T(8,128)(2,1)} %weights.1) | copy-start | bytes 1572868
  4.4 0.7 %copy-start.6 = (s32[2048]{0:T(1024)S(1)}, s32[2048]{0:T(1024)}, u32[]{:S(2)}) copy-start(s32[2048]{0:T(1024)} %neuron_s.1) | copy-start | bytes 24580
  5.1 0.7 %copy-start.7 = (s32[2048]{0:T(1024)S(1)}, s32[2048]{0:T(1024)}, u32[]{:S(2)}) copy-start(s32[2048]{0:T(1024)} %tile_s.1) | copy-start | bytes 24580
  5.8 11.6 %copy-start.1 = (f32[768,768]{1,0:T(8,128)S(1)}, f32[768,768]{1,0:T(8,128)}, u32[]{:S(2)}) copy-start(f32[768,768]{1,0:T(8,128)} %self_h.1) | copy-start | bytes 7077892
  5.8 11.7 %copy-start.2 = (f32[768,768]{1,0:T(8,128)S(1)}, f32[768,768]{1,0:T(8,128)}, u32[]{:S(2)}) copy-start(f32[768,768]{1,0:T(8,128)} %prev_h.1) | copy-start | bytes 7077892
  5.8 11.7 %copy-start.3 = (f32[768,768]{1,0:T(8,128)S(1)}, f32[768,768]{1,0:T(8,128)}, u32[]{:S(2)}) copy-start(f32[768,768]{1,0:T(8,128)} %next_h.1) | copy-start | bytes 7077892
  5.8 11.7 %copy-start.5 = (f32[16,768]{1,0:T(8,128)S(1)}, f32[16,768]{1,0:T(8,128)}, u32[]{:S(2)}) copy-start(f32[16,768]{1,0:T(8,128)} %start.1) | copy-start | bytes 147460

commit v2 on v1

--- a/solution.py
+++ b/solution.py
@@ -17,60 +17,34 @@
 NT = (((1,), (1,)), ((), ()))
 
 
-def contrib_kernel(cap, neur_dev, tile_s, neuron_s, movie, weights, neuron_v, out, staged):
-    step = pl.program_id(0)
-    rows = movie.shape[0]
-    frames = out.shape[1] - 1
-
-    @pl.loop(0, rows // 16)
-    def _(r):
-        base = pl.multiple_of(r * 16, 16)
-        for f in range(frames):
-            x = movie[pl.ds(base, 16), f * LANES:(f + 1) * LANES].astype(F32)
-            staged[pl.ds((step * rows + base) * frames + f, 16, stride=frames), :] = x
-
-    @pl.when(step == pl.num_programs(0) - 1)
-    def _():
-        for d in range(out.shape[0]):
-            out[d, :frames] = jnp.zeros((frames, LANES), F32)
-            out[d, frames:] = jnp.full((1, LANES), -1.0, F32)
-        lane = lax.broadcasted_iota(jnp.int32, (frames, LANES), 1)
-        part = 32
-
-        @pl.loop(0, weights.shape[0] // LANES)
-        def _(c):
-            first = pl.multiple_of(c * LANES, LANES)
-            w = weights[pl.ds(first, LANES), :]
-            acc = jnp.zeros((frames, LANES), F32)
-            for p in range(0, LANES, part):
-                picked = [
-                    staged[pl.ds(pl.multiple_of(tile_s[first + p + i] * frames, frames), frames), :].astype(BF16)
-                    for i in range(part)
-                ]
-                prod = lax.dot_general(jnp.concatenate(picked, axis=0), w, NT, preferred_element_type=F32)
-                for i in range(part):
-                    acc = jnp.where(lane == p + i, prod[i * frames:(i + 1) * frames], acc)
-            names = neuron_v[pl.ds(c, 1), :].astype(F32)
-            for q in range(0, LANES, cap):
-                owner = neuron_s[first + q] // neur_dev
-                out[owner, :frames] = acc
-                out[owner, frames:] = names
-
-
 def halves(x):
     hi = x.astype(BF16)
     return hi, (x - hi.astype(F32)).astype(BF16)
 
 
-def sweep_kernel(
+def trace_kernel(
     n,
     n_rows,
-    slots,
+    cap,
+    tile_h,
+    neuron_h,
+    names_h,
+    movie_h,
+    weights_h,
     self_h,
     prev_h,
     next_h,
+    start_h,
+    traces,
+    tile_s,
+    neuron_s,
+    names_v,
+    weights,
     start,
-    traces,
+    movie,
+    staged,
+    contrib,
+    slots,
     landed,
     raw,
     high,
@@ -80,8 +54,9 @@
     current,
     before,
     after,
+    small_sem,
+    movie_sem,
     raw_sem,
-    own_sem,
     send_sem,
     recv_sem,
     near_send,
@@ -93,17 +68,63 @@
     def place(d):
         return (d // n_rows, lax.rem(d, n_rows))
 
+    small = [
+        pltpu.make_async_copy(h, v, small_sem.at[i])
+        for i, (h, v) in enumerate((
+            (tile_h, tile_s), (neuron_h, neuron_s), (names_h, names_v), (weights_h, weights), (start_h, start)))
+    ]
+    tiles = movie.shape[0]
+    rows = tiles // STEPS
+
+    def piece(i):
+        part = pl.ds(pl.multiple_of(i * rows, rows), rows)
+        return pltpu.make_async_copy(movie_h.at[part], movie.at[part], movie_sem.at[i])
+
+    for i in range(STEPS):
+        piece(i).start()
+    for copy in small:
+        copy.start()
     loads = [pltpu.make_async_copy(h, raw.at[i], raw_sem.at[i]) for i, h in enumerate((self_h, prev_h, next_h))]
     for load in loads:
         load.start()
-    own = pltpu.make_async_copy(slots.at[me], landed.at[me], own_sem)
-    own.start()
 
     barrier = pltpu.get_barrier_semaphore()
 
     @pl.loop(1, n)
     def _(off):
         pl.semaphore_signal(barrier, inc=1, device_id=place(lax.rem(me + off, n)), device_id_type=MESH)
+
+    @pl.loop(0, STEPS)
+    def _(i):
+        piece(i).wait()
+
+        @pl.loop(0, rows // 16)
+        def _(r):
+            base = pl.multiple_of(i * rows + r * 16, 16)
+            for f in range(frames):
+                x = movie[pl.ds(base, 16), f * LANES:(f + 1) * LANES].astype(F32)
+                staged[pl.ds(base, 16), f, :] = x
+
+    for copy in small:
+        copy.wait()
+    lane = lax.broadcasted_iota(jnp.int32, (frames, LANES), 1)
+    part = 32
+
+    @pl.loop(0, weights.shape[0] // LANES)
+    def _(c):
+        first = pl.multiple_of(c * LANES, LANES)
+        w = weights[pl.ds(first, LANES), :]
+        acc = jnp.zeros((frames, LANES), F32)
+        for p in range(0, LANES, part):
+            picked = [
+                staged[tile_s[first + p + i]].astype(BF16)
+                for i in range(part)
+            ]
+            prod = lax.dot_general(jnp.concatenate(picked, axis=0), w, NT, preferred_element_type=F32)
+            for i in range(part):
+                acc = jnp.where(lane == p + i, prod[i * frames:(i + 1) * frames], acc)
+        contrib[c, :frames] = acc
+        contrib[c, frames:] = names_v[pl.ds(c, 1), :].astype(F32)
 
     pl.semaphore_wait(barrier, n - 1)
 
@@ -153,6 +174,17 @@
             to_prev(src, k).wait_send()
 
     share(start, 0)
+
+    def group_of(d):
+        low_end = d * neur_dev
+        found = 0
+        for head in range(0, tile_s.shape[0], cap):
+            name = neuron_s[head]
+            mine = jnp.logical_and(name >= low_end, name < low_end + neur_dev)
+            found = jnp.where(mine, head // LANES, found)
+        return found
+
+    landed[me] = contrib[0]
 
     def slot_copy(off):
         d = lax.rem(me + off, n)
@@ -162,6 +194,8 @@
 
     @pl.loop(1, n)
     def _(off):
+        d = lax.rem(me + off, n)
+        slots[d] = contrib[group_of(d)]
         slot_copy(off).start()
 
     eye = lax.broadcasted_iota(jnp.int32, (LANES, LANES), 0) == lax.broadcasted_iota(jnp.int32, (LANES, LANES), 1)
@@ -192,7 +226,6 @@
     projected[...] = jnp.zeros_like(projected)
     number = lax.broadcasted_iota(jnp.int32, (neur_dev, LANES), 0).astype(F32)
     shift = (me * neur_dev).astype(F32)
-    own.wait()
 
     @pl.loop(0, n // BATCH)
     def _(b):
@@ -250,31 +283,24 @@
     entries = entry_tile.shape[0]
     tiles = movie.shape[0]
     cap = 2 * entries // n
-    whole = pl.BlockSpec(memory_space=pltpu.VMEM)
-    scalar = pl.BlockSpec(memory_space=pltpu.SMEM)
     anywhere = pl.BlockSpec(memory_space=pl.ANY)
-    slots = pl.pallas_call(
-        functools.partial(contrib_kernel, cap, neur_dev),
-        grid=(STEPS,),
-        in_specs=[
-            scalar,
-            scalar,
-            pl.BlockSpec((tiles // STEPS, frames * LANES), lambda i: (i, 0)),
-            whole,
-            whole,
-        ],
-        out_specs=pl.BlockSpec((n, frames + 1, LANES), lambda i: (0, 0, 0)),
-        out_shape=jax.ShapeDtypeStruct((n, frames + 1, LANES), F32),
-        scratch_shapes=[pltpu.VMEM((tiles * frames, LANES), F32)],
-        compiler_params=pltpu.CompilerParams(vmem_limit_bytes=40 * 2**20),
-        name="contrib",
-    )(entry_tile, entry_neuron, movie, entry_weights, entry_neuron.reshape(entries // LANES, LANES))
+    chunks = entries // LANES
+    voxels = entry_weights.shape[1]
     return pl.pallas_call(
-        functools.partial(sweep_kernel, n, n_rows),
-        in_specs=[anywhere] * 4 + [whole],
-        out_specs=whole,
+        functools.partial(trace_kernel, n, n_rows, cap),
+        in_specs=[anywhere] * 9,
+        out_specs=pl.BlockSpec(memory_space=pltpu.VMEM),
         out_shape=jax.ShapeDtypeStruct((frames, neur_dev), F32),
         scratch_shapes=[
+            pltpu.SMEM((entries,), jnp.int32),
+            pltpu.SMEM((entries,), jnp.int32),
+            pltpu.VMEM((chunks, LANES), jnp.int32),
+            pltpu.VMEM((entries, voxels), BF16),
+            pltpu.VMEM((frames, neur_dev), F32),
+            pltpu.VMEM((tiles, frames * voxels), BF16),
+            pltpu.VMEM((tiles, frames, LANES), F32),
+            pltpu.VMEM((chunks, frames + 1, LANES), F32),
+            pltpu.VMEM((n, frames + 1, LANES), F32),
             pltpu.VMEM((n, frames + 1, LANES), F32),
             pltpu.VMEM((3, neur_dev, neur_dev), F32),
             pltpu.VMEM((3, neur_dev, neur_dev), BF16),
@@ -284,17 +310,28 @@
             pltpu.VMEM((SWEEPS - 1, frames, neur_dev), F32),
             pltpu.VMEM((SWEEPS, frames, neur_dev), F32),
             pltpu.VMEM((SWEEPS, frames, neur_dev), F32),
+            pltpu.SemaphoreType.DMA((5,)),
+            pltpu.SemaphoreType.DMA((STEPS,)),
             pltpu.SemaphoreType.DMA((3,)),
-            pltpu.SemaphoreType.DMA,
             pltpu.SemaphoreType.DMA((n,)),
             pltpu.SemaphoreType.DMA((n,)),
             pltpu.SemaphoreType.DMA((2, SWEEPS)),
             pltpu.SemaphoreType.DMA((2, SWEEPS)),
         ],
         compiler_params=pltpu.CompilerParams(
-            vmem_limit_bytes=40 * 2**20, collective_id=0, has_side_effects=True),
-        name="sweeps",
-    )(slots, intersection_self, intersection_prev, intersection_next, prev_traces)
+            vmem_limit_bytes=60 * 2**20, collective_id=0, has_side_effects=True),
+        name="traces",
+    )(
+        entry_tile,
+        entry_neuron,
+        entry_neuron.reshape(chunks, LANES),
+        movie,
+        entry_weights,
+        intersection_self,
+        intersection_prev,
+        intersection_next,
+        prev_traces,
+    )
 
 
 def solution(mesh):

time: 44.1 us -> 40.5 us (0.918)
  local copies, waits for them, and re-layouts: 6.45 us -> 1.42 us
  Pallas kernels: 37.4 us -> 38.8 us
    unnamed x17 -> x1, local copies, waits for them, and re-layouts: 6.45 us -> 1.42 us
    pallas_call x2 -> x1, Pallas kernels: 37.4 us -> 38.8 us  [local(): pl.pallas_call(functools.partial(trace_kernel, n, n_rows, cap), in_specs=...]
where the time goes in v2:
time: 40.5 us; the launch traced here: 40.2 us
  Pallas kernels  38.8 us (96%)
  local copies, waits for them, and re-layouts  1.42 us (4%)
    pallas_call x1, Pallas kernels, local(): pl.pallas_call(functools.partial(trace_kernel, n, n_rows, cap), in_specs=...  38.8 us
    unnamed x1, local copies, waits for them, and re-layouts  1.42 us

profile of v2, /device:TPU:7, one launch (start us, length us, event | category | flops | bytes accessed | tf_op | source)
XLA Modules:
  0.0 40.2 jit_solution(2417890667421809185)
XLA Ops:
  0.0 38.8 %traces.1 = f32[16,768]{1,0:T(8,128)} custom-call(s32[2048]{0:T(1024)} %tile_h.1, s32[2048]{0:T(1024)} %neuron_h.1, s32[16,128]{1,0:T(8,128)} %bitcast.1, bf16[2048,2048]{1,0:T(8,128)(2,1)} %movie_h.1, bf16[2048,128]{1,0:T(8,128)(2,1)} %weights_h.1, f32[768,768]{1,0:T(8,128)} %self_h.1, f32[768,768]{1,0:T(8,128)} %prev_h.1, f32[768,768]{1,0:T(8,128)} %next_h.1, ...), custom_call_target="tpu_custom_call" | custom-call | tf_op jit(solution)/shard_map/traces/pallas_call | solution.py:289
  38.8 1.4 %copy.10 = f32[16,768]{1,0:T(8,128)} copy(f32[16,768]{1,0:T(8,128)} %traces.1) | data formatting | bytes 98304

commit v3 on v2

--- a/solution.py
+++ b/solution.py
@@ -94,6 +94,8 @@
     def _(off):
         pl.semaphore_signal(barrier, inc=1, device_id=place(lax.rem(me + off, n)), device_id_type=MESH)
 
+    flat = staged.reshape(tiles * frames, LANES)
+
     @pl.loop(0, STEPS)
     def _(i):
         piece(i).wait()
@@ -103,77 +105,27 @@
             base = pl.multiple_of(i * rows + r * 16, 16)
             for f in range(frames):
                 x = movie[pl.ds(base, 16), f * LANES:(f + 1) * LANES].astype(F32)
-                staged[pl.ds(base, 16), f, :] = x
+                flat[pl.ds(base * frames + f, 16, stride=frames), :] = x
 
     for copy in small:
         copy.wait()
     lane = lax.broadcasted_iota(jnp.int32, (frames, LANES), 1)
     part = 32
 
-    @pl.loop(0, weights.shape[0] // LANES)
-    def _(c):
-        first = pl.multiple_of(c * LANES, LANES)
-        w = weights[pl.ds(first, LANES), :]
-        acc = jnp.zeros((frames, LANES), F32)
-        for p in range(0, LANES, part):
-            picked = [
-                staged[tile_s[first + p + i]].astype(BF16)
-                for i in range(part)
-            ]
-            prod = lax.dot_general(jnp.concatenate(picked, axis=0), w, NT, preferred_element_type=F32)
-            for i in range(part):
-                acc = jnp.where(lane == p + i, prod[i * frames:(i + 1) * frames], acc)
-        contrib[c, :frames] = acc
-        contrib[c, frames:] = names_v[pl.ds(c, 1), :].astype(F32)
-
-    pl.semaphore_wait(barrier, n - 1)
-
-    def to_next(src, k):
-        return pltpu.make_async_remote_copy(
-            src_ref=src, dst_ref=before.at[k], send_sem=near_send.at[0, k], recv_sem=near_recv.at[0, k],
-            device_id=place(lax.rem(me + 1, n)), device_id_type=MESH)
-
-    def to_prev(src, k):
-        return pltpu.make_async_remote_copy(
-            src_ref=src, dst_ref=after.at[k], send_sem=near_send.at[1, k], recv_sem=near_recv.at[1, k],
-            device_id=place(lax.rem(me + n - 1, n)), device_id_type=MESH)
-
-    def share(src, k):
-        @pl.when(me < n - 1)
-        def _():
-            to_next(src, k).start()
-
-        @pl.when(me > 0)
-        def _():
-            to_prev(src, k).start()
-
-    def receive(src, k):
-        @pl.when(me > 0)
-        def _():
-            to_next(src, k).wait_recv()
-
-        @pl.when(me < n - 1)
-        def _():
-            to_prev(src, k).wait_recv()
-
-        @pl.when(me == 0)
-        def _():
-            before[k] = jnp.zeros((frames, neur_dev), F32)
-
-        @pl.when(me == n - 1)
-        def _():
-            after[k] = jnp.zeros((frames, neur_dev), F32)
-
-    def sent(src, k):
-        @pl.when(me < n - 1)
-        def _():
-            to_next(src, k).wait_send()
-
-        @pl.when(me > 0)
-        def _():
-            to_prev(src, k).wait_send()
-
-    share(start, 0)
+    @pl.loop(0, weights.shape[0] // (2 * LANES))
+    def _(pair):
+        for half in range(2):
+            c = pair * 2 + half
+            first = pl.multiple_of(c * LANES, LANES)
+            w = weights[pl.ds(first, LANES), :].astype(F32).T.astype(BF16)
+            acc = jnp.zeros((frames, LANES), F32)
+            for p in range(0, LANES, part):
+                picked = [staged[tile_s[first + p + i]].astype(BF16) for i in range(part)]
+                prod = jnp.dot(jnp.concatenate(picked, axis=0), w, preferred_element_type=F32)
+                for i in range(part):
+                    acc = jnp.where(lane == p + i, prod[i * frames:(i + 1) * frames], acc)
+            contrib[c, :frames] = acc
+            contrib[c, frames:] = names_v[pl.ds(c, 1), :].astype(F32)
 
     def group_of(d):
         low_end = d * neur_dev
@@ -186,6 +138,60 @@
 
     landed[me] = contrib[0]
 
+    @pl.loop(1, n)
+    def _(off):
+        d = lax.rem(me + off, n)
+        slots[d] = contrib[group_of(d)]
+
+    pl.semaphore_wait(barrier, n - 1)
+
+    def to_next(src, k):
+        return pltpu.make_async_remote_copy(
+            src_ref=src, dst_ref=before.at[k], send_sem=near_send.at[0, k], recv_sem=near_recv.at[0, k],
+            device_id=place(lax.rem(me + 1, n)), device_id_type=MESH)
+
+    def to_prev(src, k):
+        return pltpu.make_async_remote_copy(
+            src_ref=src, dst_ref=after.at[k], send_sem=near_send.at[1, k], recv_sem=near_recv.at[1, k],
+            device_id=place(lax.rem(me + n - 1, n)), device_id_type=MESH)
+
+    def share(src, k):
+        @pl.when(me < n - 1)
+        def _():
+            to_next(src, k).start()
+
+        @pl.when(me > 0)
+        def _():
+            to_prev(src, k).start()
+
+    def receive(src, k):
+        @pl.when(me > 0)
+        def _():
+            to_next(src, k).wait_recv()
+
+        @pl.when(me < n - 1)
+        def _():
+            to_prev(src, k).wait_recv()
+
+        @pl.when(me == 0)
+        def _():
+            before[k] = jnp.zeros((frames, neur_dev), F32)
+
+        @pl.when(me == n - 1)
+        def _():
+            after[k] = jnp.zeros((frames, neur_dev), F32)
+
+    def sent(src, k):
+        @pl.when(me < n - 1)
+        def _():
+            to_next(src, k).wait_send()
+
+        @pl.when(me > 0)
+        def _():
+            to_prev(src, k).wait_send()
+
+    share(start, 0)
+
     def slot_copy(off):
         d = lax.rem(me + off, n)
         return pltpu.make_async_remote_copy(
@@ -194,8 +200,6 @@
 
     @pl.loop(1, n)
     def _(off):
-        d = lax.rem(me + off, n)
-        slots[d] = contrib[group_of(d)]
         slot_copy(off).start()
 
     eye = lax.broadcasted_iota(jnp.int32, (LANES, LANES), 0) == lax.broadcasted_iota(jnp.int32, (LANES, LANES), 1)
@@ -245,10 +249,11 @@
             names = landed[source, frames:] - shift
             hots.append(jnp.where(number == names, 1.0, 0.0).astype(BF16))
             values.append(jnp.concatenate(halves(landed[source, :frames]), axis=0))
-        projected[...] += lax.dot_general(
-            jnp.concatenate(values, axis=1), jnp.concatenate(hots, axis=1), NT, preferred_element_type=F32)
-
-    total = projected[:frames] + projected[frames:]
+        projected[:, :2 * frames] += lax.dot_general(
+            jnp.concatenate(hots, axis=1), jnp.concatenate(values, axis=1), NT, preferred_element_type=F32)
+
+    sums = projected[...].T
+    total = sums[:frames] + sums[frames:2 * frames]
     scale = diag[...]
     for k in range(1, SWEEPS):
         current[k - 1] = jnp.maximum((total - coupled) / scale, 0.0)
@@ -306,7 +311,7 @@
             pltpu.VMEM((3, neur_dev, neur_dev), BF16),
             pltpu.VMEM((3, neur_dev, neur_dev), BF16),
             pltpu.VMEM((1, neur_dev), F32),
-            pltpu.VMEM((2 * frames, neur_dev), F32),
+            pltpu.VMEM((neur_dev, LANES), F32),
             pltpu.VMEM((SWEEPS - 1, frames, neur_dev), F32),
             pltpu.VMEM((SWEEPS, frames, neur_dev), F32),
             pltpu.VMEM((SWEEPS, frames, neur_dev), F32),

time: 40.5 us -> 35.9 us (0.89)
  Pallas kernels: 38.8 us -> 34.1 us
    pallas_call x1, Pallas kernels: 38.8 us -> 34.1 us  [local(): pl.pallas_call(functools.partial(trace_kernel, n, n_rows, cap), in_specs=...]
where the time goes in v3:
time: 35.9 us; the launch traced here: 35.5 us
  Pallas kernels  34.1 us (95%)
  local copies, waits for them, and re-layouts  1.42 us (4%)
    pallas_call x1, Pallas kernels, local(): pl.pallas_call(functools.partial(trace_kernel, n, n_rows, cap), in_specs=...  34.1 us
    unnamed x1, local copies, waits for them, and re-layouts  1.42 us

profile of v3, /device:TPU:7, one launch (start us, length us, event | category | flops | bytes accessed | tf_op | source)
XLA Modules:
  0.0 35.5 jit_solution(1421225347100833689)
XLA Ops:
  0.0 34.1 %traces.1 = f32[16,768]{1,0:T(8,128)} custom-call(s32[2048]{0:T(1024)} %tile_h.1, s32[2048]{0:T(1024)} %neuron_h.1, s32[16,128]{1,0:T(8,128)} %bitcast.1, bf16[2048,2048]{1,0:T(8,128)(2,1)} %movie_h.1, bf16[2048,128]{1,0:T(8,128)(2,1)} %weights_h.1, f32[768,768]{1,0:T(8,128)} %self_h.1, f32[768,768]{1,0:T(8,128)} %prev_h.1, f32[768,768]{1,0:T(8,128)} %next_h.1, ...), custom_call_target="tpu_custom_call" | custom-call | tf_op jit(solution)/shard_map/traces/pallas_call | solution.py:294
  34.1 1.4 %copy.10 = f32[16,768]{1,0:T(8,128)} copy(f32[16,768]{1,0:T(8,128)} %traces.1) | data formatting | bytes 98304

commit v4 on v3

--- a/solution.py
+++ b/solution.py
@@ -11,6 +11,7 @@
 LANES = 128
 STEPS = 8
 BATCH = 8
+ZONE = 8
 F32 = jnp.float32
 BF16 = jnp.bfloat16
 MESH = pl.DeviceIdType.MESH
@@ -38,6 +39,7 @@
     traces,
     tile_s,
     neuron_s,
+    chunk_of,
     names_v,
     weights,
     start,
@@ -84,6 +86,20 @@
         piece(i).start()
     for copy in small:
         copy.start()
+    zones = n // ZONE
+    zone, member = lax.div(me, ZONE), lax.rem(me, ZONE)
+
+    def turn(k):
+        return lax.rem(lax.div(k, ZONE) + 1, zones), lax.rem(lax.rem(k, ZONE) + 1, ZONE)
+
+    def target(k):
+        a, b = turn(k)
+        return lax.rem(zone + a, zones) * ZONE + lax.rem(member + b, ZONE)
+
+    def origin(k):
+        a, b = turn(k)
+        return lax.rem(zone + zones - a, zones) * ZONE + lax.rem(member + ZONE - b, ZONE)
+
     loads = [pltpu.make_async_copy(h, raw.at[i], raw_sem.at[i]) for i, h in enumerate((self_h, prev_h, next_h))]
     for load in loads:
         load.start()
@@ -112,8 +128,22 @@
     lane = lax.broadcasted_iota(jnp.int32, (frames, LANES), 1)
     part = 32
 
-    @pl.loop(0, weights.shape[0] // (2 * LANES))
+    def group_of(d):
+        low_end = d * neur_dev
+        found = 0
+        for head in range(0, tile_s.shape[0], cap):
+            name = neuron_s[head]
+            mine = jnp.logical_and(name >= low_end, name < low_end + neur_dev)
+            found = jnp.where(mine, head // LANES, found)
+        return found
+
+    pairs = weights.shape[0] // (2 * LANES)
+
+    @pl.loop(0, pairs)
     def _(pair):
+        for j in range(n // pairs):
+            d = pair * (n // pairs) + j
+            chunk_of[d] = group_of(d)
         for half in range(2):
             c = pair * 2 + half
             first = pl.multiple_of(c * LANES, LANES)
@@ -127,21 +157,9 @@
             contrib[c, :frames] = acc
             contrib[c, frames:] = names_v[pl.ds(c, 1), :].astype(F32)
 
-    def group_of(d):
-        low_end = d * neur_dev
-        found = 0
-        for head in range(0, tile_s.shape[0], cap):
-            name = neuron_s[head]
-            mine = jnp.logical_and(name >= low_end, name < low_end + neur_dev)
-            found = jnp.where(mine, head // LANES, found)
-        return found
-
+    for d in range(n):
+        slots[d] = contrib[chunk_of[d]]
     landed[me] = contrib[0]
-
-    @pl.loop(1, n)
-    def _(off):
-        d = lax.rem(me + off, n)
-        slots[d] = contrib[group_of(d)]
 
     pl.semaphore_wait(barrier, n - 1)
 
@@ -164,18 +182,19 @@
         def _():
             to_prev(src, k).start()
 
-    def receive(src, k):
+    def receive_before(src, k):
         @pl.when(me > 0)
         def _():
             to_next(src, k).wait_recv()
 
+        @pl.when(me == 0)
+        def _():
+            before[k] = jnp.zeros((frames, neur_dev), F32)
+
+    def receive_after(src, k):
         @pl.when(me < n - 1)
         def _():
             to_prev(src, k).wait_recv()
-
-        @pl.when(me == 0)
-        def _():
-            before[k] = jnp.zeros((frames, neur_dev), F32)
 
         @pl.when(me == n - 1)
         def _():
@@ -192,15 +211,15 @@
 
     share(start, 0)
 
-    def slot_copy(off):
-        d = lax.rem(me + off, n)
+    def slot_copy(k):
+        d = target(k)
         return pltpu.make_async_remote_copy(
             src_ref=slots.at[d], dst_ref=landed.at[me], send_sem=send_sem.at[d], recv_sem=recv_sem.at[me],
             device_id=place(d), device_id_type=MESH)
 
-    @pl.loop(1, n)
-    def _(off):
-        slot_copy(off).start()
+    @pl.loop(0, n - 1)
+    def _(k):
+        slot_copy(k).start()
 
     eye = lax.broadcasted_iota(jnp.int32, (LANES, LANES), 0) == lax.broadcasted_iota(jnp.int32, (LANES, LANES), 1)
     for m in range(3):
@@ -224,7 +243,8 @@
         small = jnp.dot(hi, low[m], preferred_element_type=F32)
         return both[:frames] + (both[frames:] + small)
 
-    receive(start, 0)
+    receive_before(start, 0)
+    receive_after(start, 0)
     coupled = product(start[...], 0) + product(before[0], 1) + product(after[0], 2)
 
     projected[...] = jnp.zeros_like(projected)
@@ -235,17 +255,17 @@
     def _(b):
         hots, values = [], []
         for s in range(BATCH):
-            off = b * BATCH + s
-            source = lax.rem(me + n - off, n)
-
-            @pl.when(off > 0)
+            k = b * BATCH + s
+            source = origin(k)
+
+            @pl.when(k < n - 1)
             def _():
                 pltpu.make_async_remote_copy(
                     src_ref=slots.at[source], dst_ref=landed.at[source], send_sem=send_sem.at[source],
                     recv_sem=recv_sem.at[source], device_id=place(source), device_id_type=MESH).wait_recv()
 
         for s in range(BATCH):
-            source = lax.rem(me + n - (b * BATCH + s), n)
+            source = origin(b * BATCH + s)
             names = landed[source, frames:] - shift
             hots.append(jnp.where(number == names, 1.0, 0.0).astype(BF16))
             values.append(jnp.concatenate(halves(landed[source, :frames]), axis=0))
@@ -259,17 +279,19 @@
         current[k - 1] = jnp.maximum((total - coupled) / scale, 0.0)
         share(current.at[k - 1], k)
         coupled = product(current[k - 1], 0)
-        receive(current.at[k - 1], k)
-        coupled = coupled + product(before[k], 1) + product(after[k], 2)
+        receive_before(current.at[k - 1], k)
+        coupled = coupled + product(before[k], 1)
+        receive_after(current.at[k - 1], k)
+        coupled = coupled + product(after[k], 2)
     traces[...] = jnp.maximum((total - coupled) / scale, 0.0)
 
     sent(start, 0)
     for k in range(1, SWEEPS):
         sent(current.at[k - 1], k)
 
-    @pl.loop(1, n)
-    def _(off):
-        slot_copy(off).wait_send()
+    @pl.loop(0, n - 1)
+    def _(k):
+        slot_copy(k).wait_send()
 
 
 def local(
@@ -299,6 +321,7 @@
         scratch_shapes=[
             pltpu.SMEM((entries,), jnp.int32),
             pltpu.SMEM((entries,), jnp.int32),
+            pltpu.SMEM((n,), jnp.int32),
             pltpu.VMEM((chunks, LANES), jnp.int32),
             pltpu.VMEM((entries, voxels), BF16),
             pltpu.VMEM((frames, neur_dev), F32),

time: 35.9 us -> 35 us (0.975)
  Pallas kernels: 34.1 us -> 33.4 us
    pallas_call x1, Pallas kernels: 34.1 us -> 33.4 us  [local(): pl.pallas_call(functools.partial(trace_kernel, n, n_rows, cap), in_specs=...]
where the time goes in v4:
time: 35 us; the launch traced here: 34.8 us
  Pallas kernels  33.4 us (95%)
  local copies, waits for them, and re-layouts  1.42 us (4%)
    pallas_call x1, Pallas kernels, local(): pl.pallas_call(functools.partial(trace_kernel, n, n_rows, cap), in_specs=...  33.4 us
    unnamed x1, local copies, waits for them, and re-layouts  1.42 us

profile of v4, /device:TPU:7, one launch (start us, length us, event | category | flops | bytes accessed | tf_op | source)
XLA Modules:
  0.0 34.8 jit_solution(18039497323713954354)
XLA Ops:
  0.0 33.4 %traces.1 = f32[16,768]{1,0:T(8,128)} custom-call(s32[2048]{0:T(1024)} %tile_h.1, s32[2048]{0:T(1024)} %neuron_h.1, s32[16,128]{1,0:T(8,128)} %bitcast.1, bf16[2048,2048]{1,0:T(8,128)(2,1)} %movie_h.1, bf16[2048,128]{1,0:T(8,128)(2,1)} %weights_h.1, f32[768,768]{1,0:T(8,128)} %self_h.1, f32[768,768]{1,0:T(8,128)} %prev_h.1, f32[768,768]{1,0:T(8,128)} %next_h.1, ...), custom_call_target="tpu_custom_call" | custom-call | tf_op jit(solution)/shard_map/traces/pallas_call | solution.py:316
  33.4 1.4 %copy.10 = f32[16,768]{1,0:T(8,128)} copy(f32[16,768]{1,0:T(8,128)} %traces.1) | data formatting | bytes 98304

commit v5 on v4

--- a/solution.py
+++ b/solution.py
@@ -116,12 +116,13 @@
     def _(i):
         piece(i).wait()
 
-        @pl.loop(0, rows // 16)
+        @pl.loop(0, rows // 64)
         def _(r):
-            base = pl.multiple_of(i * rows + r * 16, 16)
-            for f in range(frames):
-                x = movie[pl.ds(base, 16), f * LANES:(f + 1) * LANES].astype(F32)
-                flat[pl.ds(base * frames + f, 16, stride=frames), :] = x
+            for q in range(0, 64, 16):
+                base = pl.multiple_of(i * rows + r * 64 + q, 16)
+                for f in range(frames):
+                    x = movie[pl.ds(base, 16), f * LANES:(f + 1) * LANES].astype(F32)
+                    flat[pl.ds(base * frames + f, 16, stride=frames), :] = x
 
     for copy in small:
         copy.wait()
@@ -230,9 +231,9 @@
                 diag[:, b:b + LANES] = jnp.sum(jnp.where(eye, block, 0.0), axis=0, keepdims=True)
                 raw[0, b:b + LANES, b:b + LANES] = jnp.where(eye, 0.0, block)
 
-        @pl.loop(0, neur_dev // 16)
+        @pl.loop(0, neur_dev // 64)
         def _(r):
-            rows = pl.ds(pl.multiple_of(r * 16, 16), 16)
+            rows = pl.ds(pl.multiple_of(r * 64, 64), 64)
             hi, lo = halves(raw[m, rows, :])
             high[m, rows, :] = hi
             low[m, rows, :] = lo
@@ -279,19 +280,21 @@
         current[k - 1] = jnp.maximum((total - coupled) / scale, 0.0)
         share(current.at[k - 1], k)
         coupled = product(current[k - 1], 0)
+        if k == 1:
+            sent(start, 0)
+
+            @pl.loop(0, n - 1)
+            def _(i):
+                slot_copy(i).wait_send()
+
         receive_before(current.at[k - 1], k)
         coupled = coupled + product(before[k], 1)
         receive_after(current.at[k - 1], k)
         coupled = coupled + product(after[k], 2)
     traces[...] = jnp.maximum((total - coupled) / scale, 0.0)
 
-    sent(start, 0)
     for k in range(1, SWEEPS):
         sent(current.at[k - 1], k)
-
-    @pl.loop(0, n - 1)
-    def _(k):
-        slot_copy(k).wait_send()
 
 
 def local(

time: 35 us -> 33.9 us (0.969)
  Pallas kernels: 33.4 us -> 32.3 us
    pallas_call x1, Pallas kernels: 33.4 us -> 32.3 us  [local(): pl.pallas_call(functools.partial(trace_kernel, n, n_rows, cap), in_specs=...]
where the time goes in v5:
time: 33.9 us; the launch traced here: 33.7 us
  Pallas kernels  32.3 us (95%)
  local copies, waits for them, and re-layouts  1.42 us (4%)
    pallas_call x1, Pallas kernels, local(): pl.pallas_call(functools.partial(trace_kernel, n, n_rows, cap), in_specs=...  32.3 us
    unnamed x1, local copies, waits for them, and re-layouts  1.42 us

profile of v5, /device:TPU:7, one launch (start us, length us, event | category | flops | bytes accessed | tf_op | source)
XLA Modules:
  0.0 33.7 jit_solution(14285072834592970360)
XLA Ops:
  0.0 32.3 %traces.1 = f32[16,768]{1,0:T(8,128)} custom-call(s32[2048]{0:T(1024)} %tile_h.1, s32[2048]{0:T(1024)} %neuron_h.1, s32[16,128]{1,0:T(8,128)} %bitcast.1, bf16[2048,2048]{1,0:T(8,128)(2,1)} %movie_h.1, bf16[2048,128]{1,0:T(8,128)(2,1)} %weights_h.1, f32[768,768]{1,0:T(8,128)} %self_h.1, f32[768,768]{1,0:T(8,128)} %prev_h.1, f32[768,768]{1,0:T(8,128)} %next_h.1, ...), custom_call_target="tpu_custom_call" | custom-call | tf_op jit(solution)/shard_map/traces/pallas_call | solution.py:319
  32.3 1.4 %copy.10 = f32[16,768]{1,0:T(8,128)} copy(f32[16,768]{1,0:T(8,128)} %traces.1) | data formatting | bytes 98304

commit v6 on v5

--- a/solution.py
+++ b/solution.py
@@ -9,7 +9,7 @@
 
 SWEEPS = 3
 LANES = 128
-STEPS = 8
+STEPS = 16
 BATCH = 8
 ZONE = 8
 F32 = jnp.float32

time: 33.9 us -> 33.8 us (level)
  no operation moved by 1% of the time
where the time goes in v6:
time: 33.8 us; the launch traced here: 33.6 us
  Pallas kernels  32.2 us (95%)
  local copies, waits for them, and re-layouts  1.42 us (4%)
    pallas_call x1, Pallas kernels, local(): pl.pallas_call(functools.partial(trace_kernel, n, n_rows, cap), in_specs=...  32.2 us
    unnamed x1, local copies, waits for them, and re-layouts  1.42 us

profile of v6, /device:TPU:7, one launch (start us, length us, event | category | flops | bytes accessed | tf_op | source)
XLA Modules:
  0.0 33.6 jit_solution(4715775379010813487)
XLA Ops:
  0.0 32.2 %traces.1 = f32[16,768]{1,0:T(8,128)} custom-call(s32[2048]{0:T(1024)} %tile_h.1, s32[2048]{0:T(1024)} %neuron_h.1, s32[16,128]{1,0:T(8,128)} %bitcast.1, bf16[2048,2048]{1,0:T(8,128)(2,1)} %movie_h.1, bf16[2048,128]{1,0:T(8,128)(2,1)} %weights_h.1, f32[768,768]{1,0:T(8,128)} %self_h.1, f32[768,768]{1,0:T(8,128)} %prev_h.1, f32[768,768]{1,0:T(8,128)} %next_h.1, ...), custom_call_target="tpu_custom_call" | custom-call | tf_op jit(solution)/shard_map/traces/pallas_call | solution.py:319
  32.2 1.4 %copy.10 = f32[16,768]{1,0:T(8,128)} copy(f32[16,768]{1,0:T(8,128)} %traces.1) | data formatting | bytes 98304
